TPU v7x, 32 devices: a whole 2x2x4 slice. The times are simulated.
32 devices in a mesh: grp: 4 (over z), blk: 8 (over y, x, core).
Axes of the slice: x: 2, y: 2, z: 4, core: 2. Of those that a mesh axis runs over, the one named last changes fastest.
Arguments:
- embeddings: bfloat16 [8192, 768], P(('grp', 'blk')), may hold values from -6 to 6
- target: int32 [8192, 1], P(('grp', 'blk')), may hold values from 0 to 31; in each aligned block of 256 rows (0 to 255, 256 to 511, ...) at most 16 rows name the same one
- cluster: int32 [8192], P(('grp', 'blk')), may hold values from 0 to 15
Outputs:
- nearest: float32 [8192], P(('grp', 'blk'))
Inputs may be any that keep to these rules, and one draw needn't show every extreme that they name: The rows of one device send at most 16 rows to any one target.
All inputs are finite; a program needn't handle non-finite values.
Results may differ from a plain program's by a relative error of at most 0.0014.
Values may be sent and summed in bfloat16 or wider, within the bound.
No kernel may reach another device: no remote copies, remote signals or barrier semaphores. Data moves between devices by JAX's collectives and lax.ppermute only.
A program may use at most 64 MiB of HBM per device.

v0:
```python
import functools

import jax
import jax.numpy as jnp
from jax import lax
from jax.experimental import pallas as pl
from jax.experimental.pallas import tpu as pltpu
from jax.sharding import PartitionSpec as P

CLUSTERS = 64
TAIL = 16
VMEM = 24 << 20
VMEM_SMALL = 8 << 20


def pack_kernel(per_group, emb_ref, target_ref, cluster_ref, out_ref):
    rows, width = emb_ref.shape
    x = emb_ref[...].astype(jnp.float32)
    scale = lax.rsqrt(jnp.sum(x * x, axis=1, keepdims=True) + 1e-06)
    out_ref[:rows, :] = (x * scale).astype(jnp.bfloat16)
    key = target_ref[...] // per_group * CLUSTERS + cluster_ref[...] + 1
    key = jnp.concatenate([key, jnp.zeros((1, width - rows), jnp.int32)], axis=1)
    key = jnp.broadcast_to(key.astype(jnp.float32), (TAIL, width))
    out_ref[rows:, :] = key.astype(jnp.bfloat16)


def pack(embeddings, target, cluster, per_group):
    rows, width = embeddings.shape
    return pl.pallas_call(
        functools.partial(pack_kernel, per_group),
        out_shape=jax.ShapeDtypeStruct((rows + TAIL, width), jnp.bfloat16),
        compiler_params=pltpu.CompilerParams(vmem_limit_bytes=VMEM_SMALL),
        name="pack",
    )(embeddings, target.reshape(1, rows), cluster.reshape(1, rows))


def whole(pieces):
    return pieces[0][...] if len(pieces) == 1 else jnp.concatenate([ref[...] for ref in pieces], axis=0)


def score_plane(plane, cols, best, rows_best, want_rows, diagonal):
    rows = best[0].shape[1]
    for k, pieces in enumerate(plane):
        block = whole(pieces)
        row_keys = jnp.transpose(jnp.broadcast_to(block[rows:, :rows].astype(jnp.float32)[:1], (128, rows)))
        row_keys = jnp.concatenate([row_keys] * (rows // 128), axis=1)
        row_best = None
        for at, col_ref in enumerate(cols):
            scores = lax.dot_general(
                block[:rows], col_ref[:rows, :], (((1,), (1,)), ((), ())), preferred_element_type=jnp.float32
            )
            allowed = row_keys == col_ref[rows:, :rows].astype(jnp.float32)[:1]
            if diagonal and k == 0 and at == 0:
                one = lax.broadcasted_iota(jnp.int32, scores.shape, 0)
                other = lax.broadcasted_iota(jnp.int32, scores.shape, 1)
                allowed = allowed & (one != other)
            masked = jnp.where(allowed, scores, -1.0)
            best[at] = jnp.maximum(best[at], jnp.max(masked, axis=0, keepdims=True))
            if at in want_rows:
                for lane in range(0, rows, 128):
                    part = masked[:, lane : lane + 128]
                    row_best = part if row_best is None else jnp.maximum(row_best, part)
        if row_best is not None:
            rows_best[k] = jnp.maximum(rows_best[k], jnp.max(jnp.transpose(row_best), axis=0, keepdims=True))


def take(refs, counts):
    groups = []
    for count in counts:
        groups.append(refs[:count])
        refs = refs[count:]
    return groups


def early_kernel(counts, n_cols, *refs):
    *plane, cols, here, (twins,), (rows_out,) = take(refs, counts + (n_cols, n_cols // 2, 1, 1))
    rows = rows_out.shape[2]
    low = jnp.full((1, rows), -1.0, jnp.float32)
    best, rows_best = [low] * n_cols, [low] * len(plane)
    score_plane(plane, cols, best, rows_best, range(2, n_cols), True)
    for at in range(n_cols // 2):
        here[at][...] = best[2 * at]
        twins[at] = best[2 * at + 1]
    for k, value in enumerate(rows_best):
        rows_out[k] = value


def last_kernel(counts, ordered, *refs):
    *plane, cols, (rows_in,), (col_out,), (rows_out,) = take(refs, counts + (1, 1, 1, 1))
    rows = rows_out.shape[2]
    best = [jnp.full((1, rows), -1.0, jnp.float32)]
    rows_best = [rows_in[k] for k in range(len(plane))]
    score_plane(plane, cols, best, rows_best, (0,), False)
    col_out[...] = best[0]
    chip = lax.axis_index("blk") // 2
    for k, value in enumerate(rows_best):
        rows_out[chip ^ k if ordered else k] = value


def call(kernel, name, plane, operands, outs, n_cols):
    rows = outs[0].shape[-1]
    width = plane[0][0].shape[1]
    return pl.pallas_call(
        kernel,
        out_shape=outs,
        compiler_params=pltpu.CompilerParams(vmem_limit_bytes=VMEM),
        cost_estimate=pl.CostEstimate(
            flops=2 * len(plane) * n_cols * rows * rows * width,
            bytes_accessed=2 * (len(plane) + n_cols) * rows * width,
            transcendentals=0,
        ),
        name=name,
    )(*[piece for pieces in plane for piece in pieces], *operands)


def compare_early(plane, cols):
    rows = cols[0].shape[0] - TAIL
    n = len(cols) // 2
    counts = tuple(len(pieces) for pieces in plane)
    outs = [jax.ShapeDtypeStruct((1, rows), jnp.float32)] * n
    outs += [jax.ShapeDtypeStruct((count, 1, rows), jnp.float32) for count in (n, len(plane))]
    outs = call(functools.partial(early_kernel, counts, len(cols)), "compare_early", plane, cols, outs, len(cols))
    return outs[:n], outs[n], outs[n + 1]


def compare_last(name, plane, col, rows_best, ordered):
    rows = col.shape[0] - TAIL
    counts = tuple(len(pieces) for pieces in plane)
    outs = [jax.ShapeDtypeStruct((1, rows), jnp.float32), jax.ShapeDtypeStruct(rows_best.shape, jnp.float32)]
    return call(functools.partial(last_kernel, counts, ordered), name, plane, [col, rows_best], outs, 1)


def join_kernel(n, *refs):
    got = refs[n]
    for at in range(n):
        refs[n + 1 + at][...] = jnp.maximum(refs[at][...], got[at])


def join(here, got):
    return pl.pallas_call(
        functools.partial(join_kernel, len(here)),
        out_shape=[jax.ShapeDtypeStruct(x.shape, x.dtype) for x in here],
        compiler_params=pltpu.CompilerParams(vmem_limit_bytes=VMEM_SMALL),
        name="join",
    )(*here, got)


def plane_shift(x, mask):
    size = lax.axis_size("blk")
    return lax.ppermute(x, "blk", [(i, i ^ mask) for i in range(size)])


def fetch_planes(packed, groups):
    block, fetched, back = packed, [], []
    for shift in range(1, groups // 2 + 1):
        takers = range(groups if 2 * shift < groups else shift)
        block = lax.ppermute(block, "grp", [((z + 1) % groups, z) for z in takers])
        fetched.append(block)
        back.append([(z, (z + shift) % groups) for z in range(groups)])
    return fetched, back


def fetch_plane(packed, per_group, first):
    half = (packed.shape[0] - TAIL) // 2
    plane = {0: (packed,)}
    halves = {}
    masks = range(2, per_group, 2)
    for mask in sorted(masks, key=lambda mask: mask.bit_count()):
        low, high = mask & -mask, 1 << (mask.bit_length() - 1)
        if low == high:
            block = plane_shift(packed, mask)
            plane[mask] = (block,)
            block = lax.optimization_barrier((block, first))[0]
            halves[mask] = (block[:half], block[half:])
        else:
            plane[mask] = halves[mask] = (
                plane_shift(halves[mask ^ low][0], low),
                plane_shift(halves[mask ^ high][1], high),
            )
    return [plane[mask] for mask in range(0, per_group, 2)]


def body(embeddings, target, cluster):
    groups = lax.axis_size("grp")
    per_group = lax.axis_size("blk")
    packed = pack(embeddings, target, cluster, per_group)
    fetched, back = fetch_planes(packed, groups)
    plane = fetch_plane(packed, per_group, fetched[0])
    own_block = lax.optimization_barrier((packed, fetched[0]))[0]
    cols = []
    for block in [own_block] + fetched[:-1]:
        cols += [block, plane_shift(block, 1)]
    cols[0] = packed
    here, twins, rows_best = compare_early(plane, cols)
    here = join(here, plane_shift(twins, 1))
    last, rows_best = compare_last("compare_last", plane, fetched[-1], rows_best, False)
    last_block = lax.optimization_barrier((fetched[-1], rows_best))[0]
    twin, rows_best = compare_last("compare_twin", plane, plane_shift(last_block, 1), rows_best, True)
    here += join([last], plane_shift(twin, 1).reshape(1, *twin.shape))
    cores = [[i for i in range(per_group) if i % 2 == core] for core in range(2)]
    rows_back = lax.all_to_all(
        rows_best, "blk", split_axis=0, concat_axis=0, axis_index_groups=cores, tiled=True
    )
    found = [here[0]]
    for way, best in zip(back, here[1:]):
        found.append(lax.ppermute(best, "grp", way))
    found.append(jnp.max(rows_back, axis=0))
    return functools.reduce(jnp.maximum, found).reshape(-1)


def solution(mesh):
    return jax.shard_map(
        body,
        mesh=mesh,
        in_specs=(P(("grp", "blk"), None), P(("grp", "blk"), None), P(("grp", "blk"))),
        out_specs=P(("grp", "blk")),
        check_vma=False,
    )
```

profile of v0, /device:TPU:0, one launch (start us, length us, event | category | flops | bytes accessed | tf_op | source)
XLA Modules:
  0.0 43.6 jit_solution(16221464439924914011)
XLA Ops:
  0.0 0.7 %copy-done.2 = s32[256]{0:T(256)S(1)} copy-done((s32[256]{0:T(256)S(1)}, s32[256]{0:T(256)}, u32[]{:S(2)}) %copy-start.2) | copy-done | bytes 1048
  0.7 0.0 copy-done.1
  0.7 1.0 %copy-done = bf16[256,768]{1,0:T(8,128)(2,1)S(1)} copy-done((bf16[256,768]{1,0:T(8,128)(2,1)S(1)}, bf16[256,768]{1,0:T(8,128)(2,1)}, u32[]{:S(2)}) %copy-start) | copy-done | bytes 393240
  1.7 0.2 pack.1.refs_0_.refs_5_
  1.9 5.1 %collective-permute-start.2 = (bf16[272,768]{1,0:T(8,128)(2,1)S(1)}, bf16[272,768]{1,0:T(8,128)(2,1)S(1)}, u32[]{:S(2)}, u32[]{:S(2)}) collective-permute-start(bf16[272,768]{1,0:T(8,128)(2,1)S(1)} %pack.1.refs_0_.refs_5_), channel_id=1, source_target_pairs={{8,0},{16,8},{24,16},{0,24},{9,1},{17,9},{25,17},{1,25},{10,2},{18... | collective-permute-start | bytes 1253384 | tf_op jit(solution)/shard_map/ppermute | solution.py:157
  7.0 1.5 %collective-permute-start = (bf16[272,768]{1,0:T(8,128)(2,1)S(1)}, bf16[272,768]{1,0:T(8,128)(2,1)S(1)}, u32[]{:S(2)}, u32[]{:S(2)}) collective-permute-start(bf16[272,768]{1,0:T(8,128)(2,1)S(1)} %pack.1.refs_0_.refs_5_), channel_id=1, source_target_pairs={{0,2},{1,3},{2,0},{3,1},{4,6},{5,7},{6,4},{7,5},{8,10},{9,11},{10,... | collective-permute-start | bytes 1253384 | tf_op jit(solution)/shard_map/ppermute | solution.py:150
  8.5 1.5 %collective-permute-start.1 = (bf16[272,768]{1,0:T(8,128)(2,1)S(1)}, bf16[272,768]{1,0:T(8,128)(2,1)S(1)}, u32[]{:S(2)}, u32[]{:S(2)}) collective-permute-start(bf16[272,768]{1,0:T(8,128)(2,1)S(1)} %pack.1.refs_0_.refs_5_), channel_id=1, source_target_pairs={{0,4},{1,5},{2,6},{3,7},{4,0},{5,1},{6,2},{7,3},{8,12},{9,13},{10,... | collective-permute-start | bytes 1253384 | tf_op jit(solution)/shard_map/ppermute | solution.py:150
  10.0 5.9 %collective-permute-done.2.refs_7_ = bf16[272,768]{1,0:T(8,128)(2,1)S(1)} collective-permute-done((bf16[272,768]{1,0:T(8,128)(2,1)S(1)}, bf16[272,768]{1,0:T(8,128)(2,1)S(1)}, u32[]{:S(2)}, u32[]{:S(2)}) %collective-permute-start.2) | collective-permute-done | bytes 417824 | tf_op jit(solution)/shard_map/ppermute | solution.py:157
  15.9 0.0 collective-permute-start.5
  15.9 0.5 %collective-permute-start.6 = (bf16[272,768]{1,0:T(8,128)(2,1)S(1)}, bf16[272,768]{1,0:T(8,128)(2,1)S(1)}, u32[]{:S(2)}, u32[]{:S(2)}) collective-permute-start(bf16[272,768]{1,0:T(8,128)(2,1)S(1)} %collective-permute-done.2.refs_7_), channel_id=1, source_target_pairs={{0,1},{1,0},{2,3},{3,2},{4,5},{5,4},{6,7},{7,6},{8,9},{9,8},{10,11... | collective-permute-start | bytes 1253384 | tf_op jit(solution)/shard_map/ppermute | solution.py:150
  16.4 1.3 %collective-permute-start.9 = (bf16[272,768]{1,0:T(8,128)(2,1)S(1)}, bf16[272,768]{1,0:T(8,128)(2,1)S(1)}, u32[]{:S(2)}, u32[]{:S(2)}) collective-permute-start(bf16[272,768]{1,0:T(8,128)(2,1)S(1)} %collective-permute-done.2.refs_7_), channel_id=1, source_target_pairs={{8,0},{16,8},{9,1},{17,9},{10,2},{18,10},{11,3},{19,11},{12,4},{20... | collective-permute-start | bytes 1253384 | tf_op jit(solution)/shard_map/ppermute | solution.py:157
  17.7 0.4 collective-permute-done.refs_1_
  18.1 1.6 %collective-permute-start.4 = (bf16[144,768]{1,0:T(8,128)(2,1)S(1)}, bf16[144,768]{1,0:T(8,128)(2,1)S(1)}, u32[]{:S(2)}, u32[]{:S(2)}) collective-permute-start(bf16[144,768]{1,0:T(8,128)(2,1)S(1)} %slice.7), channel_id=1, source_target_pairs={{0,4},{1,5},{2,6},{3,7},{4,0},{5,1},{6,2},{7,3},{8,12},{9,13},{10,... | collective-permute-start | bytes 663560 | tf_op jit(solution)/shard_map/ppermute | solution.py:150
  19.7 0.0 collective-permute-done.1.refs_2_
  19.7 1.6 %collective-permute-start.3 = (bf16[128,768]{1,0:T(8,128)(2,1)S(1)}, bf16[128,768]{1,0:T(8,128)(2,1)S(1)}, u32[]{:S(2)}, u32[]{:S(2)}) collective-permute-start(bf16[128,768]{1,0:T(8,128)(2,1)S(1)} %slice.6), channel_id=1, source_target_pairs={{0,2},{1,3},{2,0},{3,1},{4,6},{5,7},{6,4},{7,5},{8,10},{9,11},{10,... | collective-permute-start | bytes 589832 | tf_op jit(solution)/shard_map/ppermute | solution.py:150
  21.2 4.7 %collective-permute-done.3.refs_3_ = bf16[128,768]{1,0:T(8,128)(2,1)S(1)} collective-permute-done((bf16[128,768]{1,0:T(8,128)(2,1)S(1)}, bf16[128,768]{1,0:T(8,128)(2,1)S(1)}, u32[]{:S(2)}, u32[]{:S(2)}) %collective-permute-start.3) | collective-permute-done | bytes 196640 | tf_op jit(solution)/shard_map/ppermute | solution.py:150
  25.9 0.0 collective-permute-done.4.refs_4_
  25.9 1.9 %compare_early.1 = (f32[1,256]{1,0:T(1,128)S(1)}, f32[1,256]{1,0:T(1,128)S(1)}, f32[2,1,256]{2,1,0:T(1,128)S(1)}, f32[4,1,256]{2,1,0:T(1,128)S(1)}) custom-call(bf16[272,768]{1,0:T(8,128)(2,1)S(1)} %pack.1.refs_0_.refs_5_, bf16[272,768]{1,0:T(8,128)(2,1)S(1)} %collective-permute-done.refs_1_, bf16[272,768]{1,0:T(8,128)(2,1)S(1)} %collective-permute-done.1.refs_2_, ...), custom_call_target="tpu_custom_call" | custom-call | flops 1610612736 | bytes 3145728 | tf_op jit(solution)/shard_map/compare_early/pallas_call | solution.py:103
  27.8 2.0 %collective-permute-done.9.refs_5_ = bf16[272,768]{1,0:T(8,128)(2,1)S(1)} collective-permute-done((bf16[272,768]{1,0:T(8,128)(2,1)S(1)}, bf16[272,768]{1,0:T(8,128)(2,1)S(1)}, u32[]{:S(2)}, u32[]{:S(2)}) %collective-permute-start.9) | collective-permute-done | bytes 417824 | tf_op jit(solution)/shard_map/ppermute | solution.py:157
  29.8 0.7 %compare_last.1 = (f32[1,256]{1,0:T(1,128)S(1)}, f32[4,1,256]{2,1,0:T(1,128)S(1)}) custom-call(bf16[272,768]{1,0:T(8,128)(2,1)S(1)} %pack.1.refs_0_.refs_5_, bf16[272,768]{1,0:T(8,128)(2,1)S(1)} %collective-permute-done.refs_1_, bf16[272,768]{1,0:T(8,128)(2,1)S(1)} %collective-permute-done.1.refs_2_, bf16[128,768]{1,0:T(8,128)(2,1)S(1)} %collective-permute-done.3.refs_3_, ...), custom_call_target="tpu_custom_call" | custom-call | flops 402653184 | bytes 1966080 | tf_op jit(solution)/shard_map/compare_last/pallas_call | solution.py:103
  30.5 0.1 collective-permute-start.10
  30.6 0.5 %collective-permute-start.7 = (f32[2,1,256]{2,1,0:T(1,128)S(1)}, f32[2,1,256]{2,1,0:T(1,128)S(1)}, u32[]{:S(2)}, u32[]{:S(2)}) collective-permute-start(f32[2,1,256]{2,1,0:T(1,128)S(1)} %get-tuple-element.24), channel_id=1, source_target_pairs={{0,1},{1,0},{2,3},{3,2},{4,5},{5,4},{6,7},{7,6},{8,9},{9,8},{10,11... | collective-permute-start | bytes 6152 | tf_op jit(solution)/shard_map/ppermute | solution.py:150
  31.1 1.2 %collective-permute-done.10.refs_5_ = bf16[272,768]{1,0:T(8,128)(2,1)S(1)} collective-permute-done((bf16[272,768]{1,0:T(8,128)(2,1)S(1)}, bf16[272,768]{1,0:T(8,128)(2,1)S(1)}, u32[]{:S(2)}, u32[]{:S(2)}) %collective-permute-start.10) | collective-permute-done | bytes 417824 | tf_op jit(solution)/shard_map/ppermute | solution.py:150
  32.4 1.3 %compare_twin.1 = (f32[1,256]{1,0:T(1,128)S(1)}, f32[4,1,256]{2,1,0:T(1,128)}) custom-call(bf16[272,768]{1,0:T(8,128)(2,1)S(1)} %pack.1.refs_0_.refs_5_, bf16[272,768]{1,0:T(8,128)(2,1)S(1)} %collective-permute-done.refs_1_, bf16[272,768]{1,0:T(8,128)(2,1)S(1)} %collective-permute-done.1.refs_2_, bf16[128,768]{1,0:T(8,128)(2,1)S(1)} %collective-permute-done.3.refs_3_, ...), custom_call_target="tpu_custom_call" | custom-call | flops 402653184 | bytes 1966080 | tf_op jit(solution)/shard_map/compare_twin/pallas_call | solution.py:103
  33.7 3.7 %all-to-all-start = ((f32[4,1,256]{2,1,0:T(1,128)}), f32[4,1,256]{2,1,0:T(1,128)S(1)}, u32[]{:S(2)}, u32[]{:S(2)}) async-start(f32[4,1,256]{2,1,0:T(1,128)} %get-tuple-element.32), calls=%async_computation | async-start | bytes 8192 | tf_op jit(solution)/shard_map/all_to_all | solution.py:201
  37.4 0.5 %collective-permute-start.8 = (f32[1,256]{1,0:T(1,128)S(1)}, f32[1,256]{1,0:T(1,128)S(1)}, u32[]{:S(2)}, u32[]{:S(2)}) collective-permute-start(f32[1,256]{1,0:T(1,128)S(1)} %get-tuple-element.26), channel_id=1, source_target_pairs={{0,8},{8,16},{16,24},{24,0},{1,9},{9,17},{17,25},{25,1},{2,10},{10... | collective-permute-start | bytes 3080 | tf_op jit(solution)/shard_map/ppermute | solution.py:206
  37.9 0.6 %collective-permute-done.11 = f32[1,256]{1,0:T(1,128)S(1)} collective-permute-done((f32[1,256]{1,0:T(1,128)S(1)}, f32[1,256]{1,0:T(1,128)S(1)}, u32[]{:S(2)}, u32[]{:S(2)}) %collective-permute-start.11) | collective-permute-done | bytes 1056 | tf_op jit(solution)/shard_map/ppermute | solution.py:150
  38.5 1.0 %collective-permute-start.12 = (f32[1,256]{1,0:T(1,128)S(1)}, f32[1,256]{1,0:T(1,128)S(1)}, u32[]{:S(2)}, u32[]{:S(2)}) collective-permute-start(f32[1,256]{1,0:T(1,128)S(1)} %join.3), channel_id=1, source_target_pairs={{0,16},{8,24},{16,0},{24,8},{1,17},{9,25},{17,1},{25,9},{2,18},{10... | collective-permute-start | bytes 3080 | tf_op jit(solution)/shard_map/ppermute | solution.py:206
  39.5 2.6 %all-to-all-done = f32[4,1,256]{2,1,0:T(1,128)S(1)} async-done(((f32[4,1,256]{2,1,0:T(1,128)}), f32[4,1,256]{2,1,0:T(1,128)S(1)}, u32[]{:S(2)}, u32[]{:S(2)}) %all-to-all-start) | async-done | bytes 4128 | tf_op jit(solution)/shard_map/all_to_all | solution.py:201
  42.1 0.7 %collective-permute-done.8 = f32[1,256]{1,0:T(1,128)S(1)} collective-permute-done((f32[1,256]{1,0:T(1,128)S(1)}, f32[1,256]{1,0:T(1,128)S(1)}, u32[]{:S(2)}, u32[]{:S(2)}) %collective-permute-start.8) | collective-permute-done | bytes 1056 | tf_op jit(solution)/shard_map/ppermute | solution.py:206
  42.8 0.2 collective-permute-done.12
  43.0 0.6 %maximum_maximum_fusion = f32[1,256]{1,0:T(1,128)} fusion(f32[1,256]{1,0:T(1,128)S(1)} %bitcast.8, f32[1,256]{1,0:T(1,128)S(1)} %collective-permute-done.12, f32[1,256]{1,0:T(1,128)S(1)} %get-tuple-element.25, f32[1,256]{1,0:T(1,128)S(1)} %collective-permute-done.8), kind=kLoop, calls=%fused_computation | loop fusion | flops 768 | bytes 5120 | tf_op jit(solution)/shard_map/max | solution.py:208
  (12 shorter events, 0.1 us)
Async XLA Ops:
  0.0 0.7 %copy-start.2 = (s32[256]{0:T(256)S(1)}, s32[256]{0:T(256)}, u32[]{:S(2)}) copy-start(s32[256]{0:T(256)} %param.5) | copy-start | bytes 3076
  0.0 0.7 %copy-start.1 = (s32[256,1]{0,1:T(1,128)S(1)}, s32[256,1]{0,1:T(1,128)}, u32[]{:S(2)}) copy-start(s32[256,1]{0,1:T(1,128)} %param.4) | copy-start | bytes 3076
  0.7 1.0 %copy-start = (bf16[256,768]{1,0:T(8,128)(2,1)S(1)}, bf16[256,768]{1,0:T(8,128)(2,1)}, u32[]{:S(2)}) copy-start(bf16[256,768]{1,0:T(8,128)(2,1)} %emb_ref.1) | copy-start | bytes 1179652
  1.9 14.0 %collective-permute-start.2 = (bf16[272,768]{1,0:T(8,128)(2,1)S(1)}, bf16[272,768]{1,0:T(8,128)(2,1)S(1)}, u32[]{:S(2)}, u32[]{:S(2)}) collective-permute-start(bf16[272,768]{1,0:T(8,128)(2,1)S(1)} %pack.1.refs_0_.refs_5_), channel_id=1, source_target_pairs={{8,0},{16,8},{24,16},{0,24},{9,1},{17,9},{25,17},{1,25},{10,2},{18... | collective-permute-start | bytes 1253384 | tf_op jit(solution)/shard_map/ppermute | solution.py:157
  7.0 11.1 %collective-permute-start = (bf16[272,768]{1,0:T(8,128)(2,1)S(1)}, bf16[272,768]{1,0:T(8,128)(2,1)S(1)}, u32[]{:S(2)}, u32[]{:S(2)}) collective-permute-start(bf16[272,768]{1,0:T(8,128)(2,1)S(1)} %pack.1.refs_0_.refs_5_), channel_id=1, source_target_pairs={{0,2},{1,3},{2,0},{3,1},{4,6},{5,7},{6,4},{7,5},{8,10},{9,11},{10,... | collective-permute-start | bytes 1253384 | tf_op jit(solution)/shard_map/ppermute | solution.py:150
  8.5 11.2 %collective-permute-start.1 = (bf16[272,768]{1,0:T(8,128)(2,1)S(1)}, bf16[272,768]{1,0:T(8,128)(2,1)S(1)}, u32[]{:S(2)}, u32[]{:S(2)}) collective-permute-start(bf16[272,768]{1,0:T(8,128)(2,1)S(1)} %pack.1.refs_0_.refs_5_), channel_id=1, source_target_pairs={{0,4},{1,5},{2,6},{3,7},{4,0},{5,1},{6,2},{7,3},{8,12},{9,13},{10,... | collective-permute-start | bytes 1253384 | tf_op jit(solution)/shard_map/ppermute | solution.py:150
  15.9 10.0 %collective-permute-start.5 = (bf16[272,768]{1,0:T(8,128)(2,1)S(1)}, bf16[272,768]{1,0:T(8,128)(2,1)S(1)}, u32[]{:S(2)}, u32[]{:S(2)}) collective-permute-start(bf16[272,768]{1,0:T(8,128)(2,1)S(1)} %pack.1.refs_0_.refs_5_), channel_id=1, source_target_pairs={{0,1},{1,0},{2,3},{3,2},{4,5},{5,4},{6,7},{7,6},{8,9},{9,8},{10,11... | collective-permute-start | bytes 1253384 | tf_op jit(solution)/shard_map/ppermute | solution.py:150
  15.9 10.0 %collective-permute-start.6 = (bf16[272,768]{1,0:T(8,128)(2,1)S(1)}, bf16[272,768]{1,0:T(8,128)(2,1)S(1)}, u32[]{:S(2)}, u32[]{:S(2)}) collective-permute-start(bf16[272,768]{1,0:T(8,128)(2,1)S(1)} %collective-permute-done.2.refs_7_), channel_id=1, source_target_pairs={{0,1},{1,0},{2,3},{3,2},{4,5},{5,4},{6,7},{7,6},{8,9},{9,8},{10,11... | collective-permute-start | bytes 1253384 | tf_op jit(solution)/shard_map/ppermute | solution.py:150
  16.4 13.4 %collective-permute-start.9 = (bf16[272,768]{1,0:T(8,128)(2,1)S(1)}, bf16[272,768]{1,0:T(8,128)(2,1)S(1)}, u32[]{:S(2)}, u32[]{:S(2)}) collective-permute-start(bf16[272,768]{1,0:T(8,128)(2,1)S(1)} %collective-permute-done.2.refs_7_), channel_id=1, source_target_pairs={{8,0},{16,8},{9,1},{17,9},{10,2},{18,10},{11,3},{19,11},{12,4},{20... | collective-permute-start | bytes 1253384 | tf_op jit(solution)/shard_map/ppermute | solution.py:157
  18.1 7.8 %collective-permute-start.4 = (bf16[144,768]{1,0:T(8,128)(2,1)S(1)}, bf16[144,768]{1,0:T(8,128)(2,1)S(1)}, u32[]{:S(2)}, u32[]{:S(2)}) collective-permute-start(bf16[144,768]{1,0:T(8,128)(2,1)S(1)} %slice.7), channel_id=1, source_target_pairs={{0,4},{1,5},{2,6},{3,7},{4,0},{5,1},{6,2},{7,3},{8,12},{9,13},{10,... | collective-permute-start | bytes 663560 | tf_op jit(solution)/shard_map/ppermute | solution.py:150
  19.7 6.2 %collective-permute-start.3 = (bf16[128,768]{1,0:T(8,128)(2,1)S(1)}, bf16[128,768]{1,0:T(8,128)(2,1)S(1)}, u32[]{:S(2)}, u32[]{:S(2)}) collective-permute-start(bf16[128,768]{1,0:T(8,128)(2,1)S(1)} %slice.6), channel_id=1, source_target_pairs={{0,2},{1,3},{2,0},{3,1},{4,6},{5,7},{6,4},{7,5},{8,10},{9,11},{10,... | collective-permute-start | bytes 589832 | tf_op jit(solution)/shard_map/ppermute | solution.py:150
  30.5 1.8 %collective-permute-start.10 = (bf16[272,768]{1,0:T(8,128)(2,1)S(1)}, bf16[272,768]{1,0:T(8,128)(2,1)S(1)}, u32[]{:S(2)}, u32[]{:S(2)}) collective-permute-start(bf16[272,768]{1,0:T(8,128)(2,1)S(1)} %collective-permute-done.9.refs_5_), channel_id=1, source_target_pairs={{0,1},{1,0},{2,3},{3,2},{4,5},{5,4},{6,7},{7,6},{8,9},{9,8},{10,11... | collective-permute-start | bytes 1253384 | tf_op jit(solution)/shard_map/ppermute | solution.py:150
  30.6 6.8 %collective-permute-start.7 = (f32[2,1,256]{2,1,0:T(1,128)S(1)}, f32[2,1,256]{2,1,0:T(1,128)S(1)}, u32[]{:S(2)}, u32[]{:S(2)}) collective-permute-start(f32[2,1,256]{2,1,0:T(1,128)S(1)} %get-tuple-element.24), channel_id=1, source_target_pairs={{0,1},{1,0},{2,3},{3,2},{4,5},{5,4},{6,7},{7,6},{8,9},{9,8},{10,11... | collective-permute-start | bytes 6152 | tf_op jit(solution)/shard_map/ppermute | solution.py:150
  33.7 8.4 %all-to-all-start = ((f32[4,1,256]{2,1,0:T(1,128)}), f32[4,1,256]{2,1,0:T(1,128)S(1)}, u32[]{:S(2)}, u32[]{:S(2)}) async-start(f32[4,1,256]{2,1,0:T(1,128)} %get-tuple-element.32), calls=%async_computation | async-start | bytes 8192 | tf_op jit(solution)/shard_map/all_to_all | solution.py:201
  37.4 1.1 %collective-permute-start.11 = (f32[1,256]{1,0:T(1,128)S(1)}, f32[1,256]{1,0:T(1,128)S(1)}, u32[]{:S(2)}, u32[]{:S(2)}) collective-permute-start(f32[1,256]{1,0:T(1,128)S(1)} %get-tuple-element.31), channel_id=1, source_target_pairs={{0,1},{1,0},{2,3},{3,2},{4,5},{5,4},{6,7},{7,6},{8,9},{9,8},{10,11... | collective-permute-start | bytes 3080 | tf_op jit(solution)/shard_map/ppermute | solution.py:150
  37.4 5.4 %collective-permute-start.8 = (f32[1,256]{1,0:T(1,128)S(1)}, f32[1,256]{1,0:T(1,128)S(1)}, u32[]{:S(2)}, u32[]{:S(2)}) collective-permute-start(f32[1,256]{1,0:T(1,128)S(1)} %get-tuple-element.26), channel_id=1, source_target_pairs={{0,8},{8,16},{16,24},{24,0},{1,9},{9,17},{17,25},{25,1},{2,10},{10... | collective-permute-start | bytes 3080 | tf_op jit(solution)/shard_map/ppermute | solution.py:206
  38.5 4.5 %collective-permute-start.12 = (f32[1,256]{1,0:T(1,128)S(1)}, f32[1,256]{1,0:T(1,128)S(1)}, u32[]{:S(2)}, u32[]{:S(2)}) collective-permute-start(f32[1,256]{1,0:T(1,128)S(1)} %join.3), channel_id=1, source_target_pairs={{0,16},{8,24},{16,0},{24,8},{1,17},{9,25},{17,1},{25,9},{2,18},{10... | collective-permute-start | bytes 3080 | tf_op jit(solution)/shard_map/ppermute | solution.py:206
where the time goes:
time: 43.8 us; the launch traced here: 43.6 us
  starting transfers between devices  18.8 us (43%)
  waiting for transfers between devices  18.3 us (42%)
  Pallas kernels  4.15 us (9%)
  local copies, waits for them, and re-layouts  1.72 us (4%)
  other arithmetic  0.59 us (1%)
    ppermute x2, waiting for transfers between devices, fetch_planes(): block = lax.ppermute(block, 'grp', [((z + 1) % groups, z) for z in takers])  7.86 us
    ppermute x9, starting transfers between devices, plane_shift(): return lax.ppermute(x, 'blk', [(i, i ^ mask) for i in range(size)])  7.23 us
    ppermute x9, waiting for transfers between devices, plane_shift(): return lax.ppermute(x, 'blk', [(i, i ^ mask) for i in range(size)])  6.92 us
    ppermute x2, starting transfers between devices, fetch_planes(): block = lax.ppermute(block, 'grp', [((z + 1) % groups, z) for z in takers])  6.38 us
    pallas_call x3, Pallas kernels, call(): pl.pallas_call(kernel, out_shape=outs, compiler_params=pltpu.CompilerPara...  3.98 us
    all_to_all x1, starting transfers between devices, body(): lax.all_to_all(rows_best, 'blk', split_axis=0, concat_axis=0, axis_index_...  3.71 us
    all_to_all x1, waiting for transfers between devices, body(): lax.all_to_all(rows_best, 'blk', split_axis=0, concat_axis=0, axis_index_...  2.57 us
    unnamed x6, local copies, waits for them, and re-layouts  1.69 us
  transfers between devices with their start and end apart: 14, of which 9 were waited for; matrix products, arithmetic and copies ran while one was open for 0% of the time, Pallas kernels for 7%

commit v1 on v0

v1 whole, which is shorter than its diff:
```python
import functools

import jax
import jax.numpy as jnp
from jax import lax
from jax.experimental import pallas as pl
from jax.experimental.pallas import tpu as pltpu
from jax.sharding import PartitionSpec as P

CLUSTERS = 64
TAIL = 16
VMEM = 24 << 20
VMEM_SMALL = 8 << 20


def pack_kernel(per_group, emb_ref, target_ref, cluster_ref, out_ref):
    rows, width = emb_ref.shape
    x = emb_ref[...].astype(jnp.float32)
    scale = lax.rsqrt(jnp.sum(x * x, axis=1, keepdims=True) + 1e-06)
    out_ref[:rows, :] = (x * scale).astype(jnp.bfloat16)
    key = target_ref[...] // per_group * CLUSTERS + cluster_ref[...] + 1
    key = jnp.concatenate([key, jnp.zeros((1, width - rows), jnp.int32)], axis=1)
    key = jnp.broadcast_to(key.astype(jnp.float32), (TAIL, width))
    out_ref[rows:, :] = key.astype(jnp.bfloat16)


def pack(embeddings, target, cluster, per_group):
    rows, width = embeddings.shape
    return pl.pallas_call(
        functools.partial(pack_kernel, per_group),
        out_shape=jax.ShapeDtypeStruct((rows + TAIL, width), jnp.bfloat16),
        compiler_params=pltpu.CompilerParams(vmem_limit_bytes=VMEM_SMALL),
        name="pack",
    )(embeddings, target.reshape(1, rows), cluster.reshape(1, rows))


def whole(pieces):
    return pieces[0][...] if len(pieces) == 1 else jnp.concatenate([ref[...] for ref in pieces], axis=0)


def score_block(pieces, cols, best, want_rows, diagonal):
    rows = best[0].shape[1]
    block = whole(pieces)
    row_keys = jnp.transpose(jnp.broadcast_to(block[rows:, :rows].astype(jnp.float32)[:1], (128, rows)))
    row_keys = jnp.concatenate([row_keys] * (rows // 128), axis=1)
    row_best = None
    for at, col_ref in enumerate(cols):
        scores = lax.dot_general(
            block[:rows], col_ref[:rows, :], (((1,), (1,)), ((), ())), preferred_element_type=jnp.float32
        )
        allowed = row_keys == col_ref[rows:, :rows].astype(jnp.float32)[:1]
        if at == diagonal:
            one = lax.broadcasted_iota(jnp.int32, scores.shape, 0)
            other = lax.broadcasted_iota(jnp.int32, scores.shape, 1)
            allowed = allowed & (one != other)
        masked = jnp.where(allowed, scores, -1.0)
        best[at] = jnp.maximum(best[at], jnp.max(masked, axis=0, keepdims=True))
        if at in want_rows:
            for lane in range(0, rows, 128):
                part = masked[:, lane : lane + 128]
                row_best = part if row_best is None else jnp.maximum(row_best, part)
    if row_best is None:
        return None
    return jnp.max(jnp.transpose(row_best), axis=0, keepdims=True)


def take(refs, counts):
    groups, at = [], 0
    for count in counts:
        groups.append(refs[at : at + count])
        at += count
    return groups


def first_kernel(counts, n_cols, *refs):
    *plane, cols, bests, (rows_out,) = take(refs, counts + (n_cols, n_cols, 1))
    best = [jnp.full((1, rows_out.shape[2]), -1.0, jnp.float32)] * n_cols
    for at, pieces in enumerate(plane):
        rows_out[at] = score_block(pieces, cols, best, range(2, n_cols), None if at else 0)
    for ref, value in zip(bests, best):
        ref[...] = value


def second_kernel(counts, masks, n_cols, *refs):
    n_here = n_cols // 2
    *plane, cols, earlier, (rows_in,), here, (twins,), (rows_out,) = take(
        refs, counts + (n_cols, n_cols, 1, n_here, 1, 1)
    )
    chip = lax.axis_index("blk") // 2
    best = [ref[...] for ref in earlier]
    n_first = rows_in.shape[0]
    for at in range(n_first):
        rows_out[chip ^ masks[at]] = rows_in[at]
    for at, pieces in enumerate(plane):
        rows_out[chip ^ masks[n_first + at]] = score_block(pieces, cols, best, range(2, n_cols), None)
    for at in range(n_here):
        here[at][...] = best[2 * at]
        twins[at] = best[2 * at + 1]


def last_kernel(counts, *refs):
    *plane, cols, (out_ref,) = take(refs, counts + (1, 1))
    best = [jnp.full(out_ref.shape, -1.0, jnp.float32)]
    for pieces in plane:
        score_block(pieces, cols, best, (), None)
    out_ref[...] = best[0]


def call(kernel, name, plane, operands, outs, n_cols):
    rows = outs[0].shape[-1]
    width = plane[0][0].shape[1]
    return pl.pallas_call(
        kernel,
        out_shape=outs,
        compiler_params=pltpu.CompilerParams(vmem_limit_bytes=VMEM),
        cost_estimate=pl.CostEstimate(
            flops=2 * len(plane) * n_cols * rows * rows * width,
            bytes_accessed=2 * (len(plane) + n_cols) * rows * width,
            transcendentals=0,
        ),
        name=name,
    )(*[piece for pieces in plane for piece in pieces], *operands)


def sizes(plane):
    return tuple(len(pieces) for pieces in plane)


def compare_first(plane, cols):
    rows = cols[0].shape[0] - TAIL
    outs = [jax.ShapeDtypeStruct((1, rows), jnp.float32)] * len(cols)
    outs += [jax.ShapeDtypeStruct((len(plane), 1, rows), jnp.float32)]
    kernel = functools.partial(first_kernel, sizes(plane), len(cols))
    *best, rows_best = call(kernel, "compare_first", plane, cols, outs, len(cols))
    return best, rows_best


def compare_second(plane, masks, cols, best, rows_best):
    rows = cols[0].shape[0] - TAIL
    n = len(cols) // 2
    outs = [jax.ShapeDtypeStruct((1, rows), jnp.float32)] * n
    outs += [jax.ShapeDtypeStruct((count, 1, rows), jnp.float32) for count in (n, len(masks))]
    kernel = functools.partial(second_kernel, sizes(plane), masks, len(cols))
    *here, twins, rows_best = call(kernel, "compare_second", plane, [*cols, *best, rows_best], outs, len(cols))
    return here, twins, rows_best


def compare_last(name, plane, col):
    outs = [jax.ShapeDtypeStruct((1, col.shape[0] - TAIL), jnp.float32)]
    return call(functools.partial(last_kernel, sizes(plane)), name, plane, [col], outs, 1)[0]


def join_kernel(n, *refs):
    got = refs[n]
    for at in range(n):
        refs[n + 1 + at][...] = jnp.maximum(refs[at][...], got[at])


def join(here, got):
    return pl.pallas_call(
        functools.partial(join_kernel, len(here)),
        out_shape=[jax.ShapeDtypeStruct(x.shape, x.dtype) for x in here],
        compiler_params=pltpu.CompilerParams(vmem_limit_bytes=VMEM_SMALL),
        name="join",
    )(*here, got)


def plane_shift(x, mask):
    size = lax.axis_size("blk")
    return lax.ppermute(x, "blk", [(i, i ^ mask) for i in range(size)])


def grp_shift(x, shift, mask=0):
    groups, size = lax.axis_size("grp"), lax.axis_size("blk")
    if not mask:
        return lax.ppermute(x, "grp", [(z, (z + shift) % groups) for z in range(groups)])
    pairs = [
        (z * size + i, (z + shift) % groups * size + (i ^ mask)) for z in range(groups) for i in range(size)
    ]
    return lax.ppermute(x, ("grp", "blk"), pairs)


def fetch_plane(packed, per_group):
    half = (packed.shape[0] - TAIL) // 2
    plane = {0: (packed,)}
    halves = {}
    for mask in sorted(range(2, per_group, 2), key=lambda mask: mask.bit_count()):
        low, high = mask & -mask, 1 << (mask.bit_length() - 1)
        if low == high:
            block = plane_shift(packed, mask)
            plane[mask] = (block,)
            halves[mask] = (block[:half], block[half:])
        else:
            plane[mask] = halves[mask] = (
                plane_shift(halves[mask ^ low][0], low),
                plane_shift(halves[mask ^ high][1], high),
            )
    return plane


def body(embeddings, target, cluster):
    groups = lax.axis_size("grp")
    per_group = lax.axis_size("blk")
    packed = pack(embeddings, target, cluster, per_group)
    fetched = [grp_shift(packed, -1)]
    plane = fetch_plane(packed, per_group)
    direct = [mask for mask, pieces in plane.items() if len(pieces) == 1]
    relayed = [mask for mask, pieces in plane.items() if len(pieces) > 1]
    own_block = lax.optimization_barrier((packed, fetched[0]))[0]
    own_twin = plane_shift(own_block, 1)
    while len(fetched) < groups // 2:
        block = lax.optimization_barrier((fetched[-1], own_twin, *[plane[mask] for mask in direct]))[0]
        fetched.append(grp_shift(block, -1))
    *fetched, last = fetched
    cols = [packed, own_twin]
    for block in fetched:
        cols += [block, plane_shift(block, 1)]
    best, rows_best = compare_first([plane[mask] for mask in direct], cols)
    masks = tuple(mask // 2 for mask in direct + relayed)
    here, twins, rows_best = compare_second([plane[mask] for mask in relayed], masks, cols, best, rows_best)
    here = join(here, plane_shift(twins, 1))
    cores = [[i for i in range(per_group) if i % 2 == core] for core in range(2)]
    rows_back = lax.all_to_all(
        rows_best, "blk", split_axis=0, concat_axis=0, axis_index_groups=cores, tiled=True
    )
    found = [here[0], jnp.max(rows_back, axis=0)]
    for shift, col_best in enumerate(here[1:], 1):
        found.append(grp_shift(col_best, shift))
    blocks = list(plane.values())
    last_then = lax.optimization_barrier((last, rows_best))[0]
    found.append(grp_shift(compare_last("compare_last", blocks, last), groups // 2))
    found.append(grp_shift(compare_last("compare_twin", blocks, plane_shift(last_then, 1)), groups // 2, 1))
    return functools.reduce(jnp.maximum, found).reshape(-1)


def solution(mesh):
    return jax.shard_map(
        body,
        mesh=mesh,
        in_specs=(P(("grp", "blk"), None), P(("grp", "blk"), None), P(("grp", "blk"))),
        out_specs=P(("grp", "blk")),
        check_vma=False,
    )
```

time: 43.8 us -> 46.3 us (1.057)
  starting transfers between devices: 18.8 us -> 23.5 us
  waiting for transfers between devices: 18.3 us -> 16 us
    ppermute x4 -> x5, starting transfers between devices: 7.86 us -> 12.8 us  [the longest x4 12.7 us: grp_shift(): lax.ppermute(x, 'grp', [(z, (z + shift) % groups) for z in range(groups)])]
    all_to_all x1, waiting for transfers between devices: 2.57 us -> 0.01 us  [body(): lax.all_to_all(rows_best, 'blk', split_axis=0, concat_axis=0, axis_index_...]
    ppermute x4 -> x5, waiting for transfers between devices: 8.77 us -> 9.73 us  [the longest x4 6.69 us: grp_shift(): lax.ppermute(x, 'grp', [(z, (z + shift) % groups) for z in range(groups)])]
    ppermute x9 -> x8, waiting for transfers between devices: 6.92 us -> 6.29 us  [plane_shift(): return lax.ppermute(x, 'blk', [(i, i ^ mask) for i in range(size)])]
    pallas_call x3 -> x4, Pallas kernels: 3.98 us -> 4.05 us  [call(): pl.pallas_call(kernel, out_shape=outs, compiler_params=pltpu.CompilerPara...]
    ppermute x9 -> x8, starting transfers between devices: 7.23 us -> 7.17 us  [plane_shift(): return lax.ppermute(x, 'blk', [(i, i ^ mask) for i in range(size)])]
  transfers between devices with their start and end apart: 14 -> 14, of which waited for: 9 -> 6; matrix products, arithmetic and copies ran while one was open for 0% -> 0% of each run, Pallas kernels for 7% -> 9%
where the time goes in v1:
time: 46.3 us; the launch traced here: 46.1 us
  starting transfers between devices  23.5 us (51%)
  waiting for transfers between devices  16 us (35%)
  Pallas kernels  4.21 us (9%)
  local copies, waits for them, and re-layouts  1.72 us (4%)
  other arithmetic  0.59 us (1%)
    ppermute x4, starting transfers between devices, grp_shift(): lax.ppermute(x, 'grp', [(z, (z + shift) % groups) for z in range(groups)])  12.7 us
    ppermute x8, starting transfers between devices, plane_shift(): return lax.ppermute(x, 'blk', [(i, i ^ mask) for i in range(size)])  7.17 us
    ppermute x4, waiting for transfers between devices, grp_shift(): lax.ppermute(x, 'grp', [(z, (z + shift) % groups) for z in range(groups)])  6.69 us
    ppermute x8, waiting for transfers between devices, plane_shift(): return lax.ppermute(x, 'blk', [(i, i ^ mask) for i in range(size)])  6.29 us
    pallas_call x4, Pallas kernels, call(): pl.pallas_call(kernel, out_shape=outs, compiler_params=pltpu.CompilerPara...  4.05 us
    all_to_all x1, starting transfers between devices, body(): lax.all_to_all(rows_best, 'blk', split_axis=0, concat_axis=0, axis_index_...  3.55 us
    ppermute x1, waiting for transfers between devices, grp_shift(): return lax.ppermute(x, ('grp', 'blk'), pairs)  3.04 us
    unnamed x6, local copies, waits for them, and re-layouts  1.69 us
  transfers between devices with their start and end apart: 14, of which 6 were waited for; matrix products, arithmetic and copies ran while one was open for 0% of the time, Pallas kernels for 9%

profile of v1, /device:TPU:0, one launch (start us, length us, event | category | flops | bytes accessed | tf_op | source)
XLA Modules:
  0.0 46.1 jit_solution(5309597564061521656)
XLA Ops:
  0.0 0.7 %copy-done.2 = s32[256]{0:T(256)S(1)} copy-done((s32[256]{0:T(256)S(1)}, s32[256]{0:T(256)}, u32[]{:S(2)}) %copy-start.2) | copy-done | bytes 1048
  0.7 0.0 copy-done.1
  0.7 1.0 %copy-done = bf16[256,768]{1,0:T(8,128)(2,1)S(1)} copy-done((bf16[256,768]{1,0:T(8,128)(2,1)S(1)}, bf16[256,768]{1,0:T(8,128)(2,1)}, u32[]{:S(2)}) %copy-start) | copy-done | bytes 393240
  1.7 0.2 pack.1.refs_0_.refs_3_.refs_2_
  1.9 5.1 %collective-permute-start.4 = (bf16[272,768]{1,0:T(8,128)(2,1)S(1)}, bf16[272,768]{1,0:T(8,128)(2,1)S(1)}, u32[]{:S(2)}, u32[]{:S(2)}) collective-permute-start(bf16[272,768]{1,0:T(8,128)(2,1)S(1)} %pack.1.refs_0_.refs_3_.refs_2_), channel_id=1, source_target_pairs={{0,24},{8,0},{16,8},{24,16},{1,25},{9,1},{17,9},{25,17},{2,26},{10... | collective-permute-start | bytes 1253384 | tf_op jit(solution)/shard_map/ppermute | solution.py:176
  7.0 1.5 %collective-permute-start.2 = (bf16[272,768]{1,0:T(8,128)(2,1)S(1)}, bf16[272,768]{1,0:T(8,128)(2,1)S(1)}, u32[]{:S(2)}, u32[]{:S(2)}) collective-permute-start(bf16[272,768]{1,0:T(8,128)(2,1)S(1)} %pack.1.refs_0_.refs_3_.refs_2_), channel_id=1, source_target_pairs={{0,2},{1,3},{2,0},{3,1},{4,6},{5,7},{6,4},{7,5},{8,10},{9,11},{10,... | collective-permute-start | bytes 1253384 | tf_op jit(solution)/shard_map/ppermute | solution.py:170
  8.5 1.5 %collective-permute-start = (bf16[272,768]{1,0:T(8,128)(2,1)S(1)}, bf16[272,768]{1,0:T(8,128)(2,1)S(1)}, u32[]{:S(2)}, u32[]{:S(2)}) collective-permute-start(bf16[272,768]{1,0:T(8,128)(2,1)S(1)} %pack.1.refs_0_.refs_3_.refs_2_), channel_id=1, source_target_pairs={{0,4},{1,5},{2,6},{3,7},{4,0},{5,1},{6,2},{7,3},{8,12},{9,13},{10,... | collective-permute-start | bytes 1253384 | tf_op jit(solution)/shard_map/ppermute | solution.py:170
  10.0 5.9 %collective-permute-done.4.refs_5_.refs_4_ = bf16[272,768]{1,0:T(8,128)(2,1)S(1)} collective-permute-done((bf16[272,768]{1,0:T(8,128)(2,1)S(1)}, bf16[272,768]{1,0:T(8,128)(2,1)S(1)}, u32[]{:S(2)}, u32[]{:S(2)}) %collective-permute-start.4) | collective-permute-done | bytes 417824 | tf_op jit(solution)/shard_map/ppermute | solution.py:176
  15.9 0.0 collective-permute-start.5
  15.9 0.5 %collective-permute-start.6 = (bf16[272,768]{1,0:T(8,128)(2,1)S(1)}, bf16[272,768]{1,0:T(8,128)(2,1)S(1)}, u32[]{:S(2)}, u32[]{:S(2)}) collective-permute-start(bf16[272,768]{1,0:T(8,128)(2,1)S(1)} %collective-permute-done.4.refs_5_.refs_4_), channel_id=1, source_target_pairs={{0,1},{1,0},{2,3},{3,2},{4,5},{5,4},{6,7},{7,6},{8,9},{9,8},{10,11... | collective-permute-start | bytes 1253384 | tf_op jit(solution)/shard_map/ppermute | solution.py:170
  16.4 1.7 %collective-permute-done.2.refs_1_ = bf16[272,768]{1,0:T(8,128)(2,1)S(1)} collective-permute-done((bf16[272,768]{1,0:T(8,128)(2,1)S(1)}, bf16[272,768]{1,0:T(8,128)(2,1)S(1)}, u32[]{:S(2)}, u32[]{:S(2)}) %collective-permute-start.2) | collective-permute-done | bytes 417824 | tf_op jit(solution)/shard_map/ppermute | solution.py:170
  18.1 1.2 %collective-permute-done.refs_2_ = bf16[272,768]{1,0:T(8,128)(2,1)S(1)} collective-permute-done((bf16[272,768]{1,0:T(8,128)(2,1)S(1)}, bf16[272,768]{1,0:T(8,128)(2,1)S(1)}, u32[]{:S(2)}, u32[]{:S(2)}) %collective-permute-start) | collective-permute-done | bytes 417824 | tf_op jit(solution)/shard_map/ppermute | solution.py:170
  19.3 2.6 %collective-permute-start.9 = (bf16[272,768]{1,0:T(8,128)(2,1)S(1)}, bf16[272,768]{1,0:T(8,128)(2,1)S(1)}, u32[]{:S(2)}, u32[]{:S(2)}) collective-permute-start(bf16[272,768]{1,0:T(8,128)(2,1)S(1)} %collective-permute-done.4.refs_5_.refs_4_), channel_id=1, source_target_pairs={{0,24},{8,0},{16,8},{24,16},{1,25},{9,1},{17,9},{25,17},{2,26},{10... | collective-permute-start | bytes 1253384 | tf_op jit(solution)/shard_map/ppermute | solution.py:176
  21.9 1.6 %collective-permute-start.3 = (bf16[144,768]{1,0:T(8,128)(2,1)S(1)}, bf16[144,768]{1,0:T(8,128)(2,1)S(1)}, u32[]{:S(2)}, u32[]{:S(2)}) collective-permute-start(bf16[144,768]{1,0:T(8,128)(2,1)S(1)} %slice.9), channel_id=1, source_target_pairs={{0,4},{1,5},{2,6},{3,7},{4,0},{5,1},{6,2},{7,3},{8,12},{9,13},{10,... | collective-permute-start | bytes 663560 | tf_op jit(solution)/shard_map/ppermute | solution.py:170
  23.5 1.6 %collective-permute-start.1 = (bf16[128,768]{1,0:T(8,128)(2,1)S(1)}, bf16[128,768]{1,0:T(8,128)(2,1)S(1)}, u32[]{:S(2)}, u32[]{:S(2)}) collective-permute-start(bf16[128,768]{1,0:T(8,128)(2,1)S(1)} %slice.8), channel_id=1, source_target_pairs={{0,2},{1,3},{2,0},{3,1},{4,6},{5,7},{6,4},{7,5},{8,10},{9,11},{10,... | collective-permute-start | bytes 589832 | tf_op jit(solution)/shard_map/ppermute | solution.py:170
  25.1 0.0 collective-permute-done.6.refs_6_.refs_5_
  25.1 1.5 %compare_first.1 = (f32[1,256]{1,0:T(1,128)S(1)}, f32[1,256]{1,0:T(1,128)S(1)}, f32[1,256]{1,0:T(1,128)S(1)}, f32[1,256]{1,0:T(1,128)S(1)}, f32[3,1,256]{2,1,0:T(1,128)S(1)}) custom-call(bf16[272,768]{1,0:T(8,128)(2,1)S(1)} %pack.1.refs_0_.refs_3_.refs_2_, bf16[272,768]{1,0:T(8,128)(2,1)S(1)} %collective-permute-done.2.refs_1_, ...), custom_call_target="tpu_custom_call" | custom-call | flops 1207959552 | bytes 2752512 | tf_op jit(solution)/shard_map/compare_first/pallas_call | solution.py:112
  26.6 3.4 %collective-permute-done.1.refs_0_.refs_3_ = bf16[128,768]{1,0:T(8,128)(2,1)S(1)} collective-permute-done((bf16[128,768]{1,0:T(8,128)(2,1)S(1)}, bf16[128,768]{1,0:T(8,128)(2,1)S(1)}, u32[]{:S(2)}, u32[]{:S(2)}) %collective-permute-start.1) | collective-permute-done | bytes 196640 | tf_op jit(solution)/shard_map/ppermute | solution.py:170
  30.0 1.3 %compare_second.1 = (f32[1,256]{1,0:T(1,128)S(1)}, f32[1,256]{1,0:T(1,128)S(1)}, f32[2,1,256]{2,1,0:T(1,128)S(1)}, f32[4,1,256]{2,1,0:T(1,128)}) custom-call(bf16[128,768]{1,0:T(8,128)(2,1)S(1)} %collective-permute-done.1.refs_0_.refs_3_, bf16[144,768]{1,0:T(8,128)(2,1)S(1)} %collective-permute-done.3.refs_1_.refs_4_, ...), custom_call_target="tpu_custom_call" | custom-call | flops 402653184 | bytes 1966080 | tf_op jit(solution)/shard_map/compare_second/pallas_call | solution.py:112
  31.3 0.0 collective-permute-done.9.refs_5_
  31.3 0.0 collective-permute-start.11
  31.3 0.5 %collective-permute-start.7 = (f32[2,1,256]{2,1,0:T(1,128)S(1)}, f32[2,1,256]{2,1,0:T(1,128)S(1)}, u32[]{:S(2)}, u32[]{:S(2)}) collective-permute-start(f32[2,1,256]{2,1,0:T(1,128)S(1)} %get-tuple-element.27), channel_id=1, source_target_pairs={{0,1},{1,0},{2,3},{3,2},{4,5},{5,4},{6,7},{7,6},{8,9},{9,8},{10,11... | collective-permute-start | bytes 6152 | tf_op jit(solution)/shard_map/ppermute | solution.py:170
  31.8 3.5 %all-to-all-start = ((f32[4,1,256]{2,1,0:T(1,128)}), f32[4,1,256]{2,1,0:T(1,128)S(1)}, u32[]{:S(2)}, u32[]{:S(2)}) async-start(f32[4,1,256]{2,1,0:T(1,128)} %get-tuple-element.29), calls=%async_computation | async-start | bytes 8192 | tf_op jit(solution)/shard_map/all_to_all | solution.py:223
  35.3 0.1 collective-permute-start.8
  35.4 0.6 %compare_last.1 = f32[1,256]{1,0:T(1,128)S(1)} custom-call(bf16[272,768]{1,0:T(8,128)(2,1)S(1)} %pack.1.refs_0_.refs_3_.refs_2_, bf16[272,768]{1,0:T(8,128)(2,1)S(1)} %collective-permute-done.2.refs_1_, bf16[272,768]{1,0:T(8,128)(2,1)S(1)} %collective-permute-done.refs_2_, bf16[128,768]{1,0:T(8,128)(2,1)S(1)} %collective-permute-done.1.refs_0_.refs_3_, ...), custom_call_target="tpu_custom_call" | custom-call | flops 402653184 | bytes 1966080 | tf_op jit(solution)/shard_map/compare_last/pallas_call | solution.py:112
  36.0 4.9 %collective-permute-start.10 = (f32[1,256]{1,0:T(1,128)S(1)}, f32[1,256]{1,0:T(1,128)S(1)}, u32[]{:S(2)}, u32[]{:S(2)}) collective-permute-start(f32[1,256]{1,0:T(1,128)S(1)} %compare_last.1), channel_id=1, source_target_pairs={{0,16},{8,24},{16,0},{24,8},{1,17},{9,25},{17,1},{25,9},{2,18},{10... | collective-permute-start | bytes 3080 | tf_op jit(solution)/shard_map/ppermute | solution.py:176
  41.0 0.6 %compare_twin.1 = f32[1,256]{1,0:T(1,128)S(1)} custom-call(bf16[272,768]{1,0:T(8,128)(2,1)S(1)} %pack.1.refs_0_.refs_3_.refs_2_, bf16[272,768]{1,0:T(8,128)(2,1)S(1)} %collective-permute-done.2.refs_1_, bf16[272,768]{1,0:T(8,128)(2,1)S(1)} %collective-permute-done.refs_2_, bf16[128,768]{1,0:T(8,128)(2,1)S(1)} %collective-permute-done.1.refs_0_.refs_3_, ...), custom_call_target="tpu_custom_call" | custom-call | flops 402653184 | bytes 1966080 | tf_op jit(solution)/shard_map/compare_twin/pallas_call | solution.py:112
  41.6 0.1 collective-permute-start.12
  41.7 0.0 collective-permute-done.8
  41.7 0.8 %collective-permute-done.10 = f32[1,256]{1,0:T(1,128)S(1)} collective-permute-done((f32[1,256]{1,0:T(1,128)S(1)}, f32[1,256]{1,0:T(1,128)S(1)}, u32[]{:S(2)}, u32[]{:S(2)}) %collective-permute-start.10) | collective-permute-done | bytes 1056 | tf_op jit(solution)/shard_map/ppermute | solution.py:176
  42.5 3.0 %collective-permute-done.12 = f32[1,256]{1,0:T(1,128)S(1)} collective-permute-done((f32[1,256]{1,0:T(1,128)S(1)}, f32[1,256]{1,0:T(1,128)S(1)}, u32[]{:S(2)}, u32[]{:S(2)}) %collective-permute-start.12) | collective-permute-done | bytes 1056 | tf_op jit(solution)/shard_map/ppermute | solution.py:180
  45.5 0.6 %maximum_maximum_fusion = f32[1,256]{1,0:T(1,128)} fusion(f32[1,256]{1,0:T(1,128)S(1)} %collective-permute-done.12, f32[1,256]{1,0:T(1,128)S(1)} %collective-permute-done.10, f32[1,256]{1,0:T(1,128)S(1)} %collective-permute-done.8, f32[1,256]{1,0:T(1,128)S(1)} %get-tuple-element.28, f32[1,256]{1,0:T(1,128)S(1)} %bitcast.6), kind=kLoop, calls=%fused_computation | loop fusion | flops 1024 | bytes 6144 | tf_op jit(solution)/shard_map/max | solution.py:233
  (12 shorter events, 0.1 us)
Async XLA Ops:
  0.0 0.7 %copy-start.2 = (s32[256]{0:T(256)S(1)}, s32[256]{0:T(256)}, u32[]{:S(2)}) copy-start(s32[256]{0:T(256)} %param.5) | copy-start | bytes 3076
  0.0 0.7 %copy-start.1 = (s32[256,1]{0,1:T(1,128)S(1)}, s32[256,1]{0,1:T(1,128)}, u32[]{:S(2)}) copy-start(s32[256,1]{0,1:T(1,128)} %param.4) | copy-start | bytes 3076
  0.7 1.0 %copy-start = (bf16[256,768]{1,0:T(8,128)(2,1)S(1)}, bf16[256,768]{1,0:T(8,128)(2,1)}, u32[]{:S(2)}) copy-start(bf16[256,768]{1,0:T(8,128)(2,1)} %emb_ref.1) | copy-start | bytes 1179652
  1.9 14.0 %collective-permute-start.4 = (bf16[272,768]{1,0:T(8,128)(2,1)S(1)}, bf16[272,768]{1,0:T(8,128)(2,1)S(1)}, u32[]{:S(2)}, u32[]{:S(2)}) collective-permute-start(bf16[272,768]{1,0:T(8,128)(2,1)S(1)} %pack.1.refs_0_.refs_3_.refs_2_), channel_id=1, source_target_pairs={{0,24},{8,0},{16,8},{24,16},{1,25},{9,1},{17,9},{25,17},{2,26},{10... | collective-permute-start | bytes 1253384 | tf_op jit(solution)/shard_map/ppermute | solution.py:176
  7.0 11.1 %collective-permute-start.2 = (bf16[272,768]{1,0:T(8,128)(2,1)S(1)}, bf16[272,768]{1,0:T(8,128)(2,1)S(1)}, u32[]{:S(2)}, u32[]{:S(2)}) collective-permute-start(bf16[272,768]{1,0:T(8,128)(2,1)S(1)} %pack.1.refs_0_.refs_3_.refs_2_), channel_id=1, source_target_pairs={{0,2},{1,3},{2,0},{3,1},{4,6},{5,7},{6,4},{7,5},{8,10},{9,11},{10,... | collective-permute-start | bytes 1253384 | tf_op jit(solution)/shard_map/ppermute | solution.py:170
  8.5 10.8 %collective-permute-start = (bf16[272,768]{1,0:T(8,128)(2,1)S(1)}, bf16[272,768]{1,0:T(8,128)(2,1)S(1)}, u32[]{:S(2)}, u32[]{:S(2)}) collective-permute-start(bf16[272,768]{1,0:T(8,128)(2,1)S(1)} %pack.1.refs_0_.refs_3_.refs_2_), channel_id=1, source_target_pairs={{0,4},{1,5},{2,6},{3,7},{4,0},{5,1},{6,2},{7,3},{8,12},{9,13},{10,... | collective-permute-start | bytes 1253384 | tf_op jit(solution)/shard_map/ppermute | solution.py:170
  15.9 3.4 %collective-permute-start.5 = (bf16[272,768]{1,0:T(8,128)(2,1)S(1)}, bf16[272,768]{1,0:T(8,128)(2,1)S(1)}, u32[]{:S(2)}, u32[]{:S(2)}) collective-permute-start(bf16[272,768]{1,0:T(8,128)(2,1)S(1)} %pack.1.refs_0_.refs_3_.refs_2_), channel_id=1, source_target_pairs={{0,1},{1,0},{2,3},{3,2},{4,5},{5,4},{6,7},{7,6},{8,9},{9,8},{10,11... | collective-permute-start | bytes 1253384 | tf_op jit(solution)/shard_map/ppermute | solution.py:170
  15.9 9.2 %collective-permute-start.6 = (bf16[272,768]{1,0:T(8,128)(2,1)S(1)}, bf16[272,768]{1,0:T(8,128)(2,1)S(1)}, u32[]{:S(2)}, u32[]{:S(2)}) collective-permute-start(bf16[272,768]{1,0:T(8,128)(2,1)S(1)} %collective-permute-done.4.refs_5_.refs_4_), channel_id=1, source_target_pairs={{0,1},{1,0},{2,3},{3,2},{4,5},{5,4},{6,7},{7,6},{8,9},{9,8},{10,11... | collective-permute-start | bytes 1253384 | tf_op jit(solution)/shard_map/ppermute | solution.py:170
  19.3 12.0 %collective-permute-start.9 = (bf16[272,768]{1,0:T(8,128)(2,1)S(1)}, bf16[272,768]{1,0:T(8,128)(2,1)S(1)}, u32[]{:S(2)}, u32[]{:S(2)}) collective-permute-start(bf16[272,768]{1,0:T(8,128)(2,1)S(1)} %collective-permute-done.4.refs_5_.refs_4_), channel_id=1, source_target_pairs={{0,24},{8,0},{16,8},{24,16},{1,25},{9,1},{17,9},{25,17},{2,26},{10... | collective-permute-start | bytes 1253384 | tf_op jit(solution)/shard_map/ppermute | solution.py:176
  21.9 8.1 %collective-permute-start.3 = (bf16[144,768]{1,0:T(8,128)(2,1)S(1)}, bf16[144,768]{1,0:T(8,128)(2,1)S(1)}, u32[]{:S(2)}, u32[]{:S(2)}) collective-permute-start(bf16[144,768]{1,0:T(8,128)(2,1)S(1)} %slice.9), channel_id=1, source_target_pairs={{0,4},{1,5},{2,6},{3,7},{4,0},{5,1},{6,2},{7,3},{8,12},{9,13},{10,... | collective-permute-start | bytes 663560 | tf_op jit(solution)/shard_map/ppermute | solution.py:170
  23.5 6.4 %collective-permute-start.1 = (bf16[128,768]{1,0:T(8,128)(2,1)S(1)}, bf16[128,768]{1,0:T(8,128)(2,1)S(1)}, u32[]{:S(2)}, u32[]{:S(2)}) collective-permute-start(bf16[128,768]{1,0:T(8,128)(2,1)S(1)} %slice.8), channel_id=1, source_target_pairs={{0,2},{1,3},{2,0},{3,1},{4,6},{5,7},{6,4},{7,5},{8,10},{9,11},{10,... | collective-permute-start | bytes 589832 | tf_op jit(solution)/shard_map/ppermute | solution.py:170
  31.3 9.7 %collective-permute-start.11 = (bf16[272,768]{1,0:T(8,128)(2,1)S(1)}, bf16[272,768]{1,0:T(8,128)(2,1)S(1)}, u32[]{:S(2)}, u32[]{:S(2)}) collective-permute-start(bf16[272,768]{1,0:T(8,128)(2,1)S(1)} %collective-permute-done.9.refs_5_), channel_id=1, source_target_pairs={{0,1},{1,0},{2,3},{3,2},{4,5},{5,4},{6,7},{7,6},{8,9},{9,8},{10,11... | collective-permute-start | bytes 1253384 | tf_op jit(solution)/shard_map/ppermute | solution.py:170
  31.3 4.1 %collective-permute-start.7 = (f32[2,1,256]{2,1,0:T(1,128)S(1)}, f32[2,1,256]{2,1,0:T(1,128)S(1)}, u32[]{:S(2)}, u32[]{:S(2)}) collective-permute-start(f32[2,1,256]{2,1,0:T(1,128)S(1)} %get-tuple-element.27), channel_id=1, source_target_pairs={{0,1},{1,0},{2,3},{3,2},{4,5},{5,4},{6,7},{7,6},{8,9},{9,8},{10,11... | collective-permute-start | bytes 6152 | tf_op jit(solution)/shard_map/ppermute | solution.py:170
  31.8 9.9 %all-to-all-start = ((f32[4,1,256]{2,1,0:T(1,128)}), f32[4,1,256]{2,1,0:T(1,128)S(1)}, u32[]{:S(2)}, u32[]{:S(2)}) async-start(f32[4,1,256]{2,1,0:T(1,128)} %get-tuple-element.29), calls=%async_computation | async-start | bytes 8192 | tf_op jit(solution)/shard_map/all_to_all | solution.py:223
  35.3 6.4 %collective-permute-start.8 = (f32[1,256]{1,0:T(1,128)S(1)}, f32[1,256]{1,0:T(1,128)S(1)}, u32[]{:S(2)}, u32[]{:S(2)}) collective-permute-start(f32[1,256]{1,0:T(1,128)S(1)} %get-tuple-element.30), channel_id=1, source_target_pairs={{0,8},{8,16},{16,24},{24,0},{1,9},{9,17},{17,25},{25,1},{2,10},{10... | collective-permute-start | bytes 3080 | tf_op jit(solution)/shard_map/ppermute | solution.py:176
  36.0 6.5 %collective-permute-start.10 = (f32[1,256]{1,0:T(1,128)S(1)}, f32[1,256]{1,0:T(1,128)S(1)}, u32[]{:S(2)}, u32[]{:S(2)}) collective-permute-start(f32[1,256]{1,0:T(1,128)S(1)} %compare_last.1), channel_id=1, source_target_pairs={{0,16},{8,24},{16,0},{24,8},{1,17},{9,25},{17,1},{25,9},{2,18},{10... | collective-permute-start | bytes 3080 | tf_op jit(solution)/shard_map/ppermute | solution.py:176
  41.6 4.0 %collective-permute-start.12 = (f32[1,256]{1,0:T(1,128)S(1)}, f32[1,256]{1,0:T(1,128)S(1)}, u32[]{:S(2)}, u32[]{:S(2)}) collective-permute-start(f32[1,256]{1,0:T(1,128)S(1)} %compare_twin.1), channel_id=1, source_target_pairs={{0,17},{1,16},{2,19},{3,18},{4,21},{5,20},{6,23},{7,22},{8,25},{9,... | collective-permute-start | bytes 3080 | tf_op jit(solution)/shard_map/ppermute | solution.py:180
